TPU v7x, 32 devices: a whole 2x2x4 slice. The times are simulated.
32 devices in a mesh: frame: 8 (over z, x), slab: 4 (over y, core).
Axes of the slice: x: 2, y: 2, z: 4, core: 2. Of those that a mesh axis runs over, the one named last changes fastest.
Arguments:
- latents: bfloat16 [16, 16, 160, 512], P('frame', 'slab'), may hold values from -20 to 20
- clip_starts: int32 [16], replicated, may hold values from 0 to 1
- w_space: bfloat16 [3, 3, 512, 512], replicated, may hold values from -0.09375 to 0.09375
- w_time: bfloat16 [3, 512, 512], replicated, may hold values from -0.15625 to 0.15625
- w_qkv: bfloat16 [512, 1536], replicated, may hold values from -0.25 to 0.25
- w_out: bfloat16 [512, 512], replicated, may hold values from -0.25 to 0.25
Outputs:
- block_out: bfloat16 [16, 16, 160, 512], P('frame', 'slab')
All inputs are finite; a program needn't handle non-finite values.
Results may differ from a plain program's by a relative error of at most 0.0065.
Values may be sent and summed in bfloat16 or wider, within the bound.
A program may use at most 64 MiB of HBM per device.

v0:
```python
import math

import jax
import jax.numpy as jnp
from jax import lax
from jax.sharding import PartitionSpec as P

HEADS = 8


def with_halo(block, sides, width):
    for axis, dim in sides:
        count = lax.axis_size(axis)
        forward = [(i, i + 1) for i in range(count - 1)]
        backward = [(target, source) for source, target in forward]
        low = lax.ppermute(
            lax.slice_in_dim(block, block.shape[dim] - width, None, axis=dim), axis, forward
        )
        high = lax.ppermute(lax.slice_in_dim(block, 0, width, axis=dim), axis, backward)
        block = jnp.concatenate([low, block, high], axis=dim)
    return block


def space_conv(padded_rows, w_space):
    frames, rows_padded, columns, channels = padded_rows.shape
    row_count = rows_padded - 2
    widened = jnp.pad(padded_rows, ((0, 0), (0, 0), (1, 1), (0, 0)))
    summed = jnp.zeros((frames * row_count * columns, channels), jnp.float32)
    for row_shift in range(3):
        for col_shift in range(3):
            source = widened[
                :, row_shift : row_shift + row_count, col_shift : col_shift + columns
            ].reshape(-1, channels)
            summed = summed + jnp.dot(
                source, w_space[row_shift, col_shift], preferred_element_type=jnp.float32
            )
    return jax.nn.silu(summed).astype(jnp.bfloat16).reshape(frames, row_count, columns, channels)


def clip_window(clip_starts):
    clip_ids = jnp.cumsum(clip_starts)
    padded = jnp.concatenate([jnp.full((2,), -1, jnp.int32), clip_ids])
    return padded


def time_conv(extended, window, w_time):
    count = extended.shape[0] - 2
    middle = extended.shape[1:-1]
    channels = extended.shape[-1]
    summed = jnp.zeros((count,) + middle + (channels,), jnp.float32)
    for offset in range(3):
        source = extended[2 - offset : 2 - offset + count].reshape(-1, channels)
        product = jnp.dot(source, w_time[offset], preferred_element_type=jnp.float32).reshape(
            (count,) + middle + (channels,)
        )
        allowed = (window[2 - offset : 2 - offset + count] == window[2:]).astype(jnp.float32)
        summed = summed + product * allowed.reshape((count,) + (1,) * (len(middle) + 1))
    return summed.astype(jnp.bfloat16)


def project(mixed_in, w_qkv):
    frames, pixels, channels = mixed_in.shape
    flattened = jnp.dot(mixed_in.reshape(-1, channels), w_qkv, preferred_element_type=jnp.float32)
    queries = flattened[:, :channels].astype(jnp.bfloat16).reshape(frames, pixels, channels)
    keys_out = (
        flattened[:, channels : 2 * channels].astype(jnp.bfloat16).reshape(frames, pixels, channels)
    )
    values = flattened[:, 2 * channels :].astype(jnp.bfloat16).reshape(frames, pixels, channels)
    return (queries, keys_out, values)


def attend(queries, keys_in, values, allowed, head_count):
    frames, pixels, channels = queries.shape
    head_size = channels // head_count
    query_f = queries.reshape(frames, pixels, head_count, head_size).astype(jnp.float32)
    key_f = keys_in.reshape(frames, pixels, head_count, head_size).astype(jnp.float32)
    value_f = values.reshape(frames, pixels, head_count, head_size).astype(jnp.float32)
    scores = jnp.einsum("iphd,jphd->phij", query_f, key_f) * (1.0 / math.sqrt(head_size))
    scores = jnp.where(allowed, scores, -1e30)
    weights = jax.nn.softmax(scores, axis=-1).astype(jnp.bfloat16)
    attended = jnp.einsum("phij,jphd->iphd", weights.astype(jnp.float32), value_f)
    return attended.reshape(frames, pixels, channels).astype(jnp.bfloat16)


def on_device(latents, clip_starts, w_space, w_time, w_qkv, w_out):
    frames, row_count, columns, channels = latents.shape
    device_count = lax.axis_size("frame")
    total_frames = clip_starts.shape[0]
    owned = row_count * columns // device_count
    padded = with_halo(latents, (("slab", 1),), 1)
    hidden = space_conv(padded, w_space)
    full_window = clip_window(clip_starts)
    clip_ids = full_window[2:]
    positions = jnp.arange(total_frames)
    allowed = (positions[None, :] <= positions[:, None]) & (clip_ids[None, :] == clip_ids[:, None])
    payload = hidden
    payload = payload.reshape(frames, device_count, owned, channels)
    arrived = lax.all_to_all(payload, "frame", split_axis=1, concat_axis=0, tiled=True)
    pixels = arrived.shape[2]
    extended = jnp.concatenate([jnp.zeros((2, 1, pixels, channels), arrived.dtype), arrived])
    arrived = time_conv(extended, full_window, w_time)
    pixels = arrived.shape[2]
    flattened = arrived.reshape(total_frames, pixels, channels)
    queries, keys_out, values = project(flattened, w_qkv)
    attended = attend(queries, keys_out, values, allowed, HEADS)
    result = jnp.dot(attended.reshape(-1, channels), w_out, preferred_element_type=jnp.float32)
    result = result.astype(jnp.bfloat16).reshape(total_frames, 1, pixels, channels)
    returned = lax.all_to_all(result, "frame", split_axis=0, concat_axis=1, tiled=True)
    returned = returned.reshape(frames, row_count, columns, channels)
    return (latents.astype(jnp.float32) + returned.astype(jnp.float32)).astype(jnp.bfloat16)


def solution(mesh):
    return jax.shard_map(
        on_device,
        mesh=mesh,
        in_specs=(P("frame", "slab", None, None), P(), P(), P(), P(), P()),
        out_specs=P("frame", "slab", None, None),
        check_vma=False,
    )
```

profile of v0, /device:TPU:0, one launch (start us, length us, event | category | flops | bytes accessed | tf_op | source)
XLA Modules:
  0.0 143.1 jit_solution(2589044964317348558)
XLA Ops:
  0.0 1.2 fusion.59
  1.2 2.4 %collective-permute-start = (bf16[2,1,160,512]{3,2,1,0:T(8,128)(2,1)S(1)}, bf16[2,1,160,512]{3,2,1,0:T(8,128)(2,1)S(1)}, u32[]{:S(2)}, u32[]{:S(2)}) collective-permute-start(bf16[2,1,160,512]{3,2,1,0:T(8,128)(2,1)S(1)} %get-tuple-element.16), channel_id=1, source_target_pairs={{0,1},{1,2},{2,3},{4,5},{5,6},{6,7},{8,9},{9,10},{10,11},{12,13},{... | collective-permute-start | bytes 983048 | tf_op jit(solution)/shard_map/ppermute | solution.py:16
  3.6 1.3 collective-permute-start.1
  4.9 0.0 collective-permute-done
  4.9 4.3 %collective-permute-done.1 = bf16[2,1,160,512]{3,2,1,0:T(8,128)(2,1)S(1)} collective-permute-done((bf16[2,1,160,512]{3,2,1,0:T(8,128)(2,1)S(1)}, bf16[2,1,160,512]{3,2,1,0:T(8,128)(2,1)S(1)}, u32[]{:S(2)}, u32[]{:S(2)}) %collective-permute-start.1) | collective-permute-done | bytes 327712 | tf_op jit(solution)/shard_map/ppermute | solution.py:19
  9.3 2.0 %fusion.19 = bf16[2,6,162,512]{3,2,1,0:T(8,128)(2,1)S(1)} fusion(bf16[2,1,160,512]{3,2,1,0:T(8,128)(2,1)S(1)} %collective-permute-done.1, bf16[2,4,160,512]{3,2,1,0:T(8,128)(2,1)} %param.6, bf16[2,1,160,512]{3,2,1,0:T(8,128)(2,1)S(1)} %collective-permute-done), kind=kLoop, calls=%fused_computation.36 | loop fusion | flops 11943936 | bytes 3956736 | tf_op jit(solution)/shard_map/concatenate | solution.py:20
  11.3 0.0 slice-start.1
  11.3 1.6 %fusion.58 = (bf16[2,4,160,512]{3,2,1,0:T(8,128)(2,1)S(1)}, bf16[2,4,160,512]{3,2,1,0:T(8,128)(2,1)S(1)}, bf16[2,4,160,512]{3,2,1,0:T(8,128)(2,1)S(1)}, bf16[2,4...) fusion(bf16[2,6,162,512]{3,2,1,0:T(8,128)(2,1)S(1)} %fusion.19), kind=kLoop, calls=%fused_computation.80 | loop fusion | bytes 15728640 | tf_op jit(solution)/shard_map/slice | solution.py:31
  12.9 0.8 fusion.38
  13.7 0.0 copy-start.2
  13.7 0.8 fusion.29
  14.6 0.5 copy-done.2
  15.0 0.2 pad_maximum_fusion
  15.3 0.9 convolution_add_fusion.6
  16.1 0.9 convolution_add_fusion.5
  17.0 0.9 convolution_add_fusion.4
  17.9 0.9 convolution_add_fusion.3
  18.7 0.9 convolution_add_fusion.2
  19.6 0.9 convolution_add_fusion.1
  20.4 1.2 multiply_convert_fusion
  21.7 0.0 copy-start.5
  21.7 1.2 copy.27
  22.9 5.8 %all-to-all-start = ((bf16[2,8,80,512]{3,2,0,1:T(8,128)(2,1)}), bf16[2,8,80,512]{3,2,0,1:T(8,128)(2,1)}, u32[]{:S(2)}, u32[]{:S(2)}) async-start(bf16[2,8,80,512]{3,2,0,1:T(8,128)(2,1)} %copy.27), calls=%async_computation | async-start | bytes 2621440 | tf_op jit(solution)/shard_map/all_to_all | solution.py:98
  28.7 0.1 copy.28
  28.8 0.1 reduce
  28.9 0.1 compare_convert_fusion.1
  29.0 0.1 fusion.52
  29.1 30.3 %all-to-all-done = bf16[2,8,80,512]{3,2,0,1:T(8,128)(2,1)} async-done(((bf16[2,8,80,512]{3,2,0,1:T(8,128)(2,1)}), bf16[2,8,80,512]{3,2,0,1:T(8,128)(2,1)}, u32[]{:S(2)}, u32[]{:S(2)}) %all-to-all-start) | async-done | bytes 1310752 | tf_op jit(solution)/shard_map/all_to_all | solution.py:98
  59.3 2.4 %fusion.21 = f32[16,80,512]{2,1,0:T(8,128)S(1)} fusion(bf16[16,1,80,512]{3,2,0,1:T(8,128)(2,1)} %bitcast.25, bf16[3,512,512]{2,1,0:T(8,128)(2,1)} %param.9), kind=kOutput, calls=%fused_computation.40 | convolution fusion | flops 671088640 | bytes 4456448 | tf_op jit(solution)/shard_map/dot_general | solution.py:53
  61.7 2.2 %fusion.27 = f32[16,80,512]{2,1,0:T(8,128)S(1)} fusion(bf16[16,80,512]{2,1,0:T(8,128)(2,1)} %bitcast.21, bf16[3,512,512]{2,1,0:T(8,128)(2,1)S(1)} %copy-done.4), kind=kOutput, calls=%fused_computation.46 | convolution fusion | flops 671088640 | bytes 4456448 | tf_op jit(solution)/shard_map/dot_general | solution.py:53
  63.9 2.2 %add_convert_fusion.1 = bf16[16,80,512]{2,1,0:T(8,128)(2,1)S(1)} fusion(f32[16,80,512]{2,1,0:T(8,128)S(1)} %fusion.27, f32[16,80,512]{2,1,0:T(8,128)S(1)} %fusion.21, bf16[16,1,80,512]{3,2,0,1:T(8,128)(2,1)} %bitcast.25, f32[16]{0:T(128)S(1)} %get-tuple-element.19, f32[16]{0:T(128)S(1)} %get-tuple-element.18, bf16[3,512,512]{2,1,0:T(8,128)(2,1)S(1)} %copy-done.4), kind=kOutput, calls=%fused_computation.29 | convolution fusion | flops 674365440 | bytes 8389632 | tf_op jit(solution)/shard_map/dot_general | solution.py:53
  66.1 2.2 %convolution_convert_fusion = bf16[1280,1536]{1,0:T(8,128)(2,1)S(1)} fusion(bf16[1280,512]{1,0:T(8,128)(2,1)S(1)} %bitcast.104, bf16[512,1536]{1,0:T(8,128)(2,1)S(1)} %copy-done), kind=kOutput, calls=%fused_computation.1 | convolution fusion | flops 2015232000 | bytes 6815744 | tf_op jit(solution)/shard_map/dot_general | solution.py:63
  68.3 1.8 %fusion.57 = (bf16[1280,512]{1,0:T(8,128)(2,1)S(1)}, bf16[1280,512]{1,0:T(8,128)(2,1)}, bf16[1280,512]{1,0:T(8,128)(2,1)}) fusion(bf16[1280,1536]{1,0:T(8,128)(2,1)S(1)} %convolution_convert_fusion), kind=kLoop, calls=%fused_computation.79 | loop fusion | bytes 7864320 | tf_op jit(solution)/shard_map/slice | solution.py:68
  70.2 4.3 %reshape.114 = bf16[16,80,8,64]{3,2,1,0:T(8,128)(2,1)} reshape(bf16[1280,512]{1,0:T(8,128)(2,1)} %get-tuple-element.7) | data formatting | bytes 2621440 | tf_op jit(solution)/shard_map/reshape;reshape | solution.py:75
  74.5 4.3 %reshape.115 = bf16[16,80,8,64]{3,2,1,0:T(8,128)(2,1)} reshape(bf16[1280,512]{1,0:T(8,128)(2,1)} %get-tuple-element.6) | data formatting | bytes 2621440 | tf_op jit(solution)/shard_map/reshape;reshape | solution.py:76
  78.8 2.4 %reshape.113 = bf16[16,80,8,64]{3,2,1,0:T(8,128)(2,1)} reshape(bf16[1280,512]{1,0:T(8,128)(2,1)S(1)} %get-tuple-element.5) | data formatting | bytes 2621440 | tf_op jit(solution)/shard_map/reshape;reshape | solution.py:77
  81.2 5.7 %fusion.5 = f32[80,8,16,16]{2,3,1,0:T(8,128)S(1)} fusion(bf16[16,80,8,64]{3,2,1,0:T(8,128)(2,1)} %reshape.115, bf16[16,80,8,64]{3,2,1,0:T(8,128)(2,1)} %reshape.114), kind=kOutput, calls=%fused_computation.20 | convolution fusion | flops 20971520 | bytes 3276800 | tf_op jit(solution)/shard_map/iphd,jphd->phij/dot_general | solution.py:78
  86.8 2.4 %fusion.60 = (f32[80,8,16]{2,1,0:T(8,128)S(1)}, f32[80,8,16,16]{2,3,1,0:T(8,128)S(1)}) fusion(f32[80,8,16,16]{2,3,1,0:T(8,128)S(1)} %fusion.5, pred[16,16]{0,1:T(8,128)(4,1)S(1)} %fusion.52), kind=kOutput, calls=%fused_computation.82 | output fusion | flops 983055 | bytes 1351936 | tf_op jit(solution)/shard_map/sub | solution.py:80
  89.3 0.0 copy-done.3
  89.3 3.4 %convert_bitcast_fusion.1 = bf16[16,80,8,64]{3,0,2,1:T(8,128)(2,1)} fusion(f32[80,8,16,16]{2,3,1,0:T(8,128)S(1)} %get-tuple-element.21, f32[80,8,16]{2,1,0:T(8,128)S(1)} %get-tuple-element.20, bf16[16,80,8,64]{3,2,1,0:T(8,128)(2,1)S(1)} %copy-done.3), kind=kOutput, calls=%fused_computation.25 | convolution fusion | flops 21954560 | bytes 3317760 | tf_op jit(solution)/shard_map/phij,jphd->iphd/dot_general | solution.py:81
  92.7 6.4 %copy.36 = bf16[16,80,8,64]{1,0,3,2:T(8,128)(2,1)} copy(bf16[16,80,8,64]{3,0,2,1:T(8,128)(2,1)} %convert_bitcast_fusion.1) | data formatting | bytes 2621440 | tf_op jit(solution)/shard_map/convert_element_type | solution.py:82
  99.1 3.8 %convert_element_type.64 = bf16[1280,512]{0,1:T(8,128)(2,1)S(1)} reshape(bf16[16,80,8,64]{1,0,3,2:T(8,128)(2,1)} %copy.36) | data formatting | bytes 2621440 | tf_op jit(solution)/shard_map/convert_element_type | solution.py:82
  102.9 0.9 convolution_convert_fusion.1
  103.8 37.0 %all_to_all.27 = bf16[16,1,80,512]{3,2,1,0:T(8,128)(2,1)S(1)} all-to-all(bf16[16,1,80,512]{3,2,1,0:T(8,128)(2,1)S(1)} %bitcast.106), channel_id=1, replica_groups=mesh['frame'=8,'slab'=4] {'frame'}, dimensions={0} | all-to-all | bytes 2621440 | tf_op jit(solution)/shard_map/all_to_all | solution.py:108
  140.8 0.3 convert_bitcast_fusion
  141.2 0.3 copy.38
  141.5 0.0 copy-start.1
  141.5 1.6 %add_convert_fusion = bf16[2,4,160,512]{3,2,1,0:T(8,128)(2,1)} fusion(f32[2,4,160,512]{3,2,1,0:T(8,128)S(1)} %bitcast.93, bf16[2,4,160,512]{3,2,1,0:T(8,128)(2,1)S(1)} %copy-done.2), kind=kLoop, calls=%fused_computation.24 | loop fusion | flops 1966080 | bytes 5242880 | tf_op jit(solution)/shard_map/convert_element_type | solution.py:110
  (14 shorter events, 0.1 us)
Async XLA Ops:
  0.0 66.1 %copy-start = (bf16[512,1536]{1,0:T(8,128)(2,1)S(1)}, bf16[512,1536]{1,0:T(8,128)(2,1)}, u32[]{:S(2)}) copy-start(bf16[512,1536]{1,0:T(8,128)(2,1)} %param.10) | copy-start | bytes 4718596
  1.2 3.7 %collective-permute-start = (bf16[2,1,160,512]{3,2,1,0:T(8,128)(2,1)S(1)}, bf16[2,1,160,512]{3,2,1,0:T(8,128)(2,1)S(1)}, u32[]{:S(2)}, u32[]{:S(2)}) collective-permute-start(bf16[2,1,160,512]{3,2,1,0:T(8,128)(2,1)S(1)} %get-tuple-element.16), channel_id=1, source_target_pairs={{0,1},{1,2},{2,3},{4,5},{5,6},{6,7},{8,9},{9,10},{10,11},{12,13},{... | collective-permute-start | bytes 983048 | tf_op jit(solution)/shard_map/ppermute | solution.py:16
  3.6 5.6 %collective-permute-start.1 = (bf16[2,1,160,512]{3,2,1,0:T(8,128)(2,1)S(1)}, bf16[2,1,160,512]{3,2,1,0:T(8,128)(2,1)S(1)}, u32[]{:S(2)}, u32[]{:S(2)}) collective-permute-start(bf16[2,1,160,512]{3,2,1,0:T(8,128)(2,1)S(1)} %get-tuple-element.17), channel_id=1, source_target_pairs={{1,0},{2,1},{3,2},{5,4},{6,5},{7,6},{9,8},{10,9},{11,10},{13,12},{... | collective-permute-start | bytes 983048 | tf_op jit(solution)/shard_map/ppermute | solution.py:19
  9.3 3.6 %slice-start = ((s8[4718592]{0:T(1024)(128)(4,1)}), s8[4194304]{0:T(1024)(128)(4,1)S(1)}, s32[]{:S(2)}) async-start(s8[4718592]{0:T(1024)(128)(4,1)} %bitcast.102), calls=%async_computation.2 | async-start | bytes 8388608
  11.3 1.6 %slice-start.1 = ((s8[4718592]{0:T(1024)(128)(4,1)}), s8[524288]{0:T(1024)(128)(4,1)S(1)}, s32[]{:S(2)}) async-start(s8[4718592]{0:T(1024)(128)(4,1)} %bitcast.102), calls=%async_computation.3 | async-start | bytes 1048576
  13.7 1.3 copy-start.2
  21.7 7.0 %copy-start.5 = (s32[16]{0:T(128)S(1)}, s32[16]{0:T(128)}, u32[]{:S(2)}) copy-start(s32[16]{0:T(128)} %param.7) | copy-start | bytes 196
  22.9 36.5 %all-to-all-start = ((bf16[2,8,80,512]{3,2,0,1:T(8,128)(2,1)}), bf16[2,8,80,512]{3,2,0,1:T(8,128)(2,1)}, u32[]{:S(2)}, u32[]{:S(2)}) async-start(bf16[2,8,80,512]{3,2,0,1:T(8,128)(2,1)} %copy.27), calls=%async_computation | async-start | bytes 2621440 | tf_op jit(solution)/shard_map/all_to_all | solution.py:98
  59.3 2.4 %copy-start.4 = (bf16[3,512,512]{2,1,0:T(8,128)(2,1)S(1)}, bf16[3,512,512]{2,1,0:T(8,128)(2,1)}, u32[]{:S(2)}) copy-start(bf16[3,512,512]{2,1,0:T(8,128)(2,1)} %param.9) | copy-start | bytes 4718596
  86.8 2.4 %copy-start.3 = (bf16[16,80,8,64]{3,2,1,0:T(8,128)(2,1)S(1)}, bf16[16,80,8,64]{3,2,1,0:T(8,128)(2,1)}, u32[]{:S(2)}) copy-start(bf16[16,80,8,64]{3,2,1,0:T(8,128)(2,1)} %reshape.113) | copy-start | bytes 3932164
  99.1 3.8 %copy-start.6 = (bf16[512,512]{1,0:T(8,128)(2,1)S(1)}, bf16[512,512]{1,0:T(8,128)(2,1)}, u32[]{:S(2)}) copy-start(bf16[512,512]{1,0:T(8,128)(2,1)} %param.11) | copy-start | bytes 1572868
  141.5 1.6 %copy-start.1 = (bf16[512,1536]{1,0:T(8,128)(2,1)S(1)}, bf16[512,1536]{1,0:T(8,128)(2,1)}, u32[]{:S(2)}) copy-start(bf16[512,1536]{1,0:T(8,128)(2,1)} %param.10) | copy-start | bytes 4718596
where the time goes:
time: 144 us; the launch traced here: 143 us
  blocking collectives  37 us (26%)
  waiting for transfers between devices  34.6 us (24%)
  local copies, waits for them, and re-layouts  27.9 us (19%)
  matrix products  27 us (19%)
  starting transfers between devices  9.48 us (7%)
  other arithmetic  6.92 us (5%)
    all_to_all x1, blocking collectives, on_device(): lax.all_to_all(result, 'frame', split_axis=0, concat_axis=1, tiled=True)  37 us
    all_to_all x1, waiting for transfers between devices, on_device(): lax.all_to_all(payload, 'frame', split_axis=1, concat_axis=0, tiled=True)  30.3 us
    convert_element_type x2, local copies, waits for them, and re-layouts, attend(): return attended.reshape(frames, pixels, channels).astype(jnp.bfloat16)  10.2 us
    dot_general x9, matrix products, space_conv(): jnp.dot(source, w_space[row_shift, col_shift], preferred_element_type=jnp...  8.04 us
    dot_general x3, matrix products, time_conv(): jnp.dot(source, w_time[offset], preferred_element_type=jnp.float32)  6.76 us
    all_to_all x1, starting transfers between devices, on_device(): lax.all_to_all(payload, 'frame', split_axis=1, concat_axis=0, tiled=True)  5.81 us
    dot_general x1, matrix products, attend(): jnp.einsum('iphd,jphd->phij', query_f, key_f) * (1.0 / math.sqrt(head_size))  5.66 us
    ppermute x1, waiting for transfers between devices, with_halo(): lax.ppermute(lax.slice_in_dim(block, 0, width, axis=dim), axis, backward)  4.33 us
  transfers between devices with their start and end apart: 3, of which 2 were waited for; matrix products, arithmetic and copies ran while one was open for 0% of the time, Pallas kernels for 0%

commit v1 on v0

--- a/solution.py
+++ b/solution.py
@@ -1,11 +1,17 @@
+import functools
 import math
 
 import jax
 import jax.numpy as jnp
 from jax import lax
+from jax.experimental import pallas as pl
+from jax.experimental.pallas import tpu as pltpu
 from jax.sharding import PartitionSpec as P
 
 HEADS = 8
+BLOCK = 16
+SHIFT = 4
+MESH = pl.DeviceIdType.MESH
 
 
 def with_halo(block, sides, width):
@@ -38,9 +44,10 @@
 
 
 def clip_window(clip_starts):
-    clip_ids = jnp.cumsum(clip_starts)
-    padded = jnp.concatenate([jnp.full((2,), -1, jnp.int32), clip_ids])
-    return padded
+    positions = jnp.arange(clip_starts.shape[0])
+    upto = positions[None, :] <= positions[:, None]
+    clip_ids = jnp.sum(jnp.where(upto, clip_starts[None, :], 0), axis=1)
+    return jnp.concatenate([jnp.full((2,), -1, jnp.int32), clip_ids])
 
 
 def time_conv(extended, window, w_time):
@@ -61,12 +68,12 @@
 def project(mixed_in, w_qkv):
     frames, pixels, channels = mixed_in.shape
     flattened = jnp.dot(mixed_in.reshape(-1, channels), w_qkv, preferred_element_type=jnp.float32)
-    queries = flattened[:, :channels].astype(jnp.bfloat16).reshape(frames, pixels, channels)
-    keys_out = (
-        flattened[:, channels : 2 * channels].astype(jnp.bfloat16).reshape(frames, pixels, channels)
+    flattened = flattened.astype(jnp.bfloat16).reshape(frames, pixels, 3 * channels)
+    return (
+        flattened[..., :channels],
+        flattened[..., channels : 2 * channels],
+        flattened[..., 2 * channels :],
     )
-    values = flattened[:, 2 * channels :].astype(jnp.bfloat16).reshape(frames, pixels, channels)
-    return (queries, keys_out, values)
 
 
 def attend(queries, keys_in, values, allowed, head_count):
@@ -82,7 +89,7 @@
     return attended.reshape(frames, pixels, channels).astype(jnp.bfloat16)
 
 
-def on_device(latents, clip_starts, w_space, w_time, w_qkv, w_out):
+def general(latents, clip_starts, w_space, w_time, w_qkv, w_out):
     frames, row_count, columns, channels = latents.shape
     device_count = lax.axis_size("frame")
     total_frames = clip_starts.shape[0]
@@ -93,13 +100,11 @@
     clip_ids = full_window[2:]
     positions = jnp.arange(total_frames)
     allowed = (positions[None, :] <= positions[:, None]) & (clip_ids[None, :] == clip_ids[:, None])
-    payload = hidden
-    payload = payload.reshape(frames, device_count, owned, channels)
+    payload = hidden.reshape(frames, device_count, owned, channels)
     arrived = lax.all_to_all(payload, "frame", split_axis=1, concat_axis=0, tiled=True)
     pixels = arrived.shape[2]
     extended = jnp.concatenate([jnp.zeros((2, 1, pixels, channels), arrived.dtype), arrived])
     arrived = time_conv(extended, full_window, w_time)
-    pixels = arrived.shape[2]
     flattened = arrived.reshape(total_frames, pixels, channels)
     queries, keys_out, values = project(flattened, w_qkv)
     attended = attend(queries, keys_out, values, allowed, HEADS)
@@ -110,6 +115,301 @@
     return (latents.astype(jnp.float32) + returned.astype(jnp.float32)).astype(jnp.bfloat16)
 
 
+def kernel(
+    n, slabs, row_count, columns, head_count,
+    lat_hbm, starts, ws_hbm, wt_hbm, wqkv_hbm, wo_hbm, out_ref,
+    x, ws, wt, wqkv, wo, hid, rx, tx, ret, bias, lag_mask, att,
+    load_sem, halo_send, halo_recv, fwd_send, fwd_recv, back_send, back_recv,
+):
+    frames, pixels, channels = lat_hbm.shape
+    total = n * frames
+    rows = total * BLOCK
+    chunks = pixels // (BLOCK * n)
+    blocks = pixels // BLOCK
+    first = columns // BLOCK
+    me = lax.axis_index("frame")
+    slab = lax.axis_index("slab")
+    up, down = lax.rem(slab + 1, slabs), lax.rem(slab + slabs - 1, slabs)
+
+    barrier = pltpu.get_barrier_semaphore()
+    for step in range(1, n):
+        pl.semaphore_signal(
+            barrier, inc=1, device_id=(lax.rem(me + step, n), slab), device_id_type=MESH
+        )
+    for other in (up, down):
+        pl.semaphore_signal(barrier, inc=1, device_id=(me, other), device_id_type=MESH)
+
+    loads = [
+        pltpu.make_async_copy(source, target, load_sem.at[i])
+        for i, (source, target) in enumerate(
+            (
+                (lat_hbm, x.at[:, columns : columns + pixels]),
+                (ws_hbm, ws),
+                (wt_hbm, wt),
+                (wqkv_hbm, wqkv),
+                (wo_hbm, wo),
+            )
+        )
+    ]
+    for load in loads:
+        load.start()
+
+    pl.semaphore_wait(barrier, n + 1)
+    halos = [
+        pltpu.make_async_remote_copy(
+            src_ref=lat_hbm.at[:, pixels - columns : pixels],
+            dst_ref=x.at[:, 0:columns],
+            send_sem=halo_send.at[0],
+            recv_sem=halo_recv.at[0],
+            device_id=(me, up),
+            device_id_type=MESH,
+        ),
+        pltpu.make_async_remote_copy(
+            src_ref=lat_hbm.at[:, 0:columns],
+            dst_ref=x.at[:, columns + pixels : 2 * columns + pixels],
+            send_sem=halo_send.at[1],
+            recv_sem=halo_recv.at[1],
+            device_id=(me, down),
+            device_id_type=MESH,
+        ),
+    ]
+    for halo in halos:
+        halo.start()
+
+    ids = []
+    for f in range(total):
+        ids.append(starts[f] if f == 0 else ids[-1] + starts[f])
+    row = lax.broadcasted_iota(jnp.int32, (rows, 1), 0)
+    col = lax.broadcasted_iota(jnp.int32, (1, rows), 1)
+    row_frame, row_pixel = lax.shift_right_logical(row, SHIFT), row & (BLOCK - 1)
+    col_frame, col_pixel = lax.shift_right_logical(col, SHIFT), col & (BLOCK - 1)
+    row_id, col_id = jnp.zeros_like(row), jnp.zeros_like(col)
+    lags = [jnp.zeros((rows, 1), jnp.float32) for _ in range(2)]
+    for f in range(total):
+        row_id = jnp.where(row_frame == f, ids[f], row_id)
+        col_id = jnp.where(col_frame == f, ids[f], col_id)
+        for lag in (1, 2):
+            if f >= lag:
+                same = jnp.where(ids[f - lag] == ids[f], 1.0, 0.0)
+                lags[lag - 1] = jnp.where(row_frame == f, same, lags[lag - 1])
+    allowed = (row_pixel == col_pixel) & (col_frame <= row_frame) & (row_id == col_id)
+    bias[...] = jnp.where(allowed, 0.0, -1e30)
+    for lag in range(2):
+        lag_mask[lag] = jnp.broadcast_to(lags[lag], (rows, channels)).astype(jnp.bfloat16)
+
+    def conv_row(r):
+        sums = []
+        for b in range(3):
+            total_b = None
+            for a in range(3):
+                source = x[:, pl.ds(pl.multiple_of((r + a) * columns, BLOCK), columns), :]
+                part = jnp.dot(
+                    source.reshape(frames * columns, channels),
+                    ws[a, b],
+                    preferred_element_type=jnp.float32,
+                )
+                total_b = part if total_b is None else total_b + part
+            sums.append(total_b)
+        place = lax.broadcasted_iota(jnp.int32, (columns, channels), 0)
+        for f in range(frames):
+            part = [s[f * columns : (f + 1) * columns] for s in sums]
+            left = jnp.where(place == 0, 0.0, pltpu.roll(part[0], 1, 0))
+            right = jnp.where(place == columns - 1, 0.0, pltpu.roll(part[2], columns - 1, 0))
+            v = part[1] + left + right
+            hid[f, pl.ds(pl.multiple_of(r * columns, BLOCK), columns), :] = (
+                v / (1.0 + jnp.exp(-v))
+            ).astype(jnp.bfloat16)
+
+    def spot(k, owner):
+        return pl.multiple_of(lax.rem(first + n * k + owner, blocks) * BLOCK, BLOCK)
+
+    def forward(k, step):
+        peer = lax.rem(me + step, n)
+        return pltpu.make_async_remote_copy(
+            src_ref=hid.at[:, pl.ds(spot(k, peer), BLOCK), :],
+            dst_ref=rx.at[k, pl.ds(me * frames, frames)],
+            send_sem=fwd_send.at[k, step],
+            recv_sem=fwd_recv.at[k, step],
+            device_id=(peer, slab),
+            device_id_type=MESH,
+        )
+
+    def backward(k, step):
+        peer = lax.rem(me + step, n)
+        return pltpu.make_async_remote_copy(
+            src_ref=tx.at[k, pl.ds(peer * frames, frames)],
+            dst_ref=ret.at[:, pl.ds(spot(k, me), BLOCK), :],
+            send_sem=back_send.at[k, step],
+            recv_sem=back_recv.at[k, step],
+            device_id=(peer, slab),
+            device_id_type=MESH,
+        )
+
+    def send_forward(k):
+        for step in range(1, n):
+            forward(k, step).start()
+        rx[k, pl.ds(me * frames, frames)] = hid[:, pl.ds(spot(k, me), BLOCK), :]
+
+    inner = (row_count - 2) * columns // (BLOCK * n)
+    loads[0].wait()
+    loads[1].wait()
+
+    @pl.loop(0, row_count - 2)
+    def _(t):
+        conv_row(t + 1)
+
+    for k in range(inner):
+        send_forward(k)
+    for halo in halos:
+        halo.wait()
+
+    @pl.when(slab == 0)
+    def _():
+        x[:, 0:columns] = jnp.zeros((frames, columns, channels), jnp.bfloat16)
+
+    @pl.when(slab == slabs - 1)
+    def _():
+        x[:, columns + pixels : 2 * columns + pixels] = jnp.zeros(
+            (frames, columns, channels), jnp.bfloat16
+        )
+
+    @pl.loop(0, 2)
+    def _(t):
+        conv_row((1 - t) * (row_count - 1))
+
+    @pl.loop(inner, chunks)
+    def _(k):
+        send_forward(k)
+
+    for load in loads[2:]:
+        load.wait()
+
+    lanes = 2 * (channels // head_count)
+    low = lax.broadcasted_iota(jnp.int32, (rows, lanes), 1) < lanes // 2
+    scale = 1.0 / math.sqrt(channels // head_count)
+
+    @pl.loop(0, chunks)
+    def _(k):
+        for step in range(1, n):
+            forward(k, step).wait_recv()
+        own = rx[k].reshape(rows, channels)
+        mixed = jnp.dot(own, wt[0], preferred_element_type=jnp.float32)
+        for lag in (1, 2):
+            gap = lag * BLOCK
+            lagged = jnp.concatenate(
+                [jnp.zeros((gap, channels), jnp.bfloat16), own[: rows - gap]], axis=0
+            )
+            mixed = mixed + jnp.dot(
+                lagged * lag_mask[lag - 1], wt[lag], preferred_element_type=jnp.float32
+            )
+        mixed = mixed.astype(jnp.bfloat16)
+        for pair in range(channels // lanes):
+            q, key, value = (
+                jnp.dot(
+                    mixed,
+                    wqkv[:, third * channels + pair * lanes : third * channels + (pair + 1) * lanes],
+                    preferred_element_type=jnp.float32,
+                ).astype(jnp.bfloat16)
+                for third in range(3)
+            )
+            outs = []
+            for half in range(2):
+                mine = low if half == 0 else jnp.logical_not(low)
+                q_half = jnp.where(mine, q, jnp.zeros_like(q))
+                s = lax.dot_general(
+                    q_half, key, (((1,), (1,)), ((), ())), preferred_element_type=jnp.float32
+                )
+                s = s * scale + bias[...]
+                e = jnp.exp(s - jnp.max(s, axis=1, keepdims=True))
+                norm = jnp.sum(e, axis=1, keepdims=True)
+                o = jnp.dot(e.astype(jnp.bfloat16), value, preferred_element_type=jnp.float32)
+                outs.append(o / norm)
+            att[:, pair * lanes : (pair + 1) * lanes] = jnp.where(low, outs[0], outs[1]).astype(
+                jnp.bfloat16
+            )
+        result = jnp.dot(att[...], wo[...], preferred_element_type=jnp.float32)
+        tx[k] = result.astype(jnp.bfloat16).reshape(total, BLOCK, channels)
+        for step in range(1, n):
+            backward(k, step).start()
+        ret[:, pl.ds(spot(k, me), BLOCK), :] = tx[k, pl.ds(me * frames, frames)]
+
+    @pl.loop(0, chunks)
+    def _(k):
+        for step in range(1, n):
+            backward(k, step).wait_recv()
+        for owner in range(n):
+            here = spot(k, owner)
+            moved = x[:, pl.ds(here + columns, BLOCK), :].astype(jnp.float32)
+            moved = moved + ret[:, pl.ds(here, BLOCK), :].astype(jnp.float32)
+            out_ref[:, pl.ds(here, BLOCK), :] = moved.astype(jnp.bfloat16)
+
+    @pl.loop(0, chunks)
+    def _(k):
+        for step in range(1, n):
+            forward(k, step).wait_send()
+            backward(k, step).wait_send()
+
+
+def fused(latents, clip_starts, w_space, w_time, w_qkv, w_out):
+    frames, row_count, columns, channels = latents.shape
+    n, slabs = lax.axis_size("frame"), lax.axis_size("slab")
+    pixels = row_count * columns
+    total = clip_starts.shape[0]
+    chunks = pixels // (BLOCK * n)
+    rows = total * BLOCK
+    bf16 = jnp.bfloat16
+    out = pl.pallas_call(
+        functools.partial(kernel, n, slabs, row_count, columns, HEADS),
+        out_shape=jax.ShapeDtypeStruct((frames, pixels, channels), bf16),
+        in_specs=[
+            pl.BlockSpec(memory_space=pl.ANY),
+            pl.BlockSpec(memory_space=pltpu.SMEM),
+        ]
+        + [pl.BlockSpec(memory_space=pl.ANY)] * 4,
+        out_specs=pl.BlockSpec(memory_space=pltpu.VMEM),
+        scratch_shapes=[
+            pltpu.VMEM((frames, pixels + 2 * columns, channels), bf16),
+            pltpu.VMEM(w_space.shape, bf16),
+            pltpu.VMEM(w_time.shape, bf16),
+            pltpu.VMEM(w_qkv.shape, bf16),
+            pltpu.VMEM(w_out.shape, bf16),
+            pltpu.VMEM((frames, pixels, channels), bf16),
+            pltpu.VMEM((chunks, total, BLOCK, channels), bf16),
+            pltpu.VMEM((chunks, total, BLOCK, channels), bf16),
+            pltpu.VMEM((frames, pixels, channels), bf16),
+            pltpu.VMEM((rows, rows), jnp.float32),
+            pltpu.VMEM((2, rows, channels), bf16),
+            pltpu.VMEM((rows, channels), bf16),
+            pltpu.SemaphoreType.DMA((5,)),
+            pltpu.SemaphoreType.DMA((2,)),
+            pltpu.SemaphoreType.DMA((2,)),
+            pltpu.SemaphoreType.DMA((chunks, n)),
+            pltpu.SemaphoreType.DMA((chunks, n)),
+            pltpu.SemaphoreType.DMA((chunks, n)),
+            pltpu.SemaphoreType.DMA((chunks, n)),
+        ],
+        compiler_params=pltpu.CompilerParams(
+            collective_id=0, has_side_effects=True, vmem_limit_bytes=40 * 2**20
+        ),
+    )(latents.reshape(frames, pixels, channels), clip_starts, w_space, w_time, w_qkv, w_out)
+    return out.reshape(latents.shape)
+
+
+def on_device(latents, clip_starts, w_space, w_time, w_qkv, w_out):
+    frames, row_count, columns, channels = latents.shape
+    n, slabs = lax.axis_size("frame"), lax.axis_size("slab")
+    fits = (
+        (row_count * columns) % (BLOCK * n) == 0
+        and columns % BLOCK == 0
+        and clip_starts.shape[0] * BLOCK <= 512
+        and slabs >= 3
+        and row_count >= 3
+        and n >= 2
+    )
+    plan = fused if fits else general
+    return plan(latents, clip_starts, w_space, w_time, w_qkv, w_out)
+
+
 def solution(mesh):
     return jax.shard_map(
         on_device,

time: 144 us -> 77.7 us (0.54)
  Pallas kernels: 0 us -> 68.2 us
  blocking collectives: 37 us -> 0 us
  waiting for transfers between devices: 34.6 us -> 0 us
  matrix products: 27 us -> 0 us
  local copies, waits for them, and re-layouts: 27.9 us -> 9.22 us
  starting transfers between devices: 9.48 us -> 0 us
  other arithmetic: 6.92 us -> 0 us
    pallas_call x0 -> x1, Pallas kernels: none -> 68.2 us  [fused(): pl.pallas_call(functools.partial(kernel, n, slabs, row_count, columns, HE...]
    all_to_all x1 -> x0, blocking collectives: 37 us -> none  [on_device(): lax.all_to_all(result, 'frame', split_axis=0, concat_axis=1, tiled=True)]
    all_to_all x1 -> x0, waiting for transfers between devices: 30.3 us -> none  [on_device(): lax.all_to_all(payload, 'frame', split_axis=1, concat_axis=0, tiled=True)]
    dot_general x16 -> x0, matrix products: 27 us -> none  [the longest x9 8.04 us: space_conv(): jnp.dot(source, w_space[row_shift, col_shift], preferred_element_type=jnp...]
    another operation x5 -> x0, local copies, waits for them, and re-layouts: 12.3 us -> none  [the longest x1 4.32 us: attend(): queries.reshape(frames, pixels, head_count, head_size).astype(jnp.float32)]
    convert_element_type x3 -> x0, local copies, waits for them, and re-layouts: 10.5 us -> none  [the longest x2 10.2 us: attend(): return attended.reshape(frames, pixels, channels).astype(jnp.bfloat16)]
    unnamed x18 -> x13, local copies, waits for them, and re-layouts: 0.51 us -> 9.22 us
    all_to_all x1 -> x0, starting transfers between devices: 5.81 us -> none  [on_device(): lax.all_to_all(payload, 'frame', split_axis=1, concat_axis=0, tiled=True)]
  transfers between devices with their start and end apart: 3 -> 0, of which waited for: 2 -> 0; matrix products, arithmetic and copies ran while one was open for 0% -> 0% of each run, Pallas kernels for 0% -> 0%
where the time goes in v1:
time: 77.7 us; the launch traced here: 77.4 us
  Pallas kernels  68.2 us (88%)
  local copies, waits for them, and re-layouts  9.22 us (12%)
    pallas_call x1, Pallas kernels, fused(): pl.pallas_call(functools.partial(kernel, n, slabs, row_count, columns, HE...  68.2 us
    unnamed x13, local copies, waits for them, and re-layouts  9.22 us

profile of v1, /device:TPU:0, one launch (start us, length us, event | category | flops | bytes accessed | tf_op | source)
XLA Modules:
  0.0 77.4 jit_solution(13970249527833314597)
XLA Ops:
  0.0 0.0 copy-start
  0.0 2.3 %copy-done = bf16[3,3,512,512]{3,2,1,0:T(8,128)(2,1)S(1)} copy-done((bf16[3,3,512,512]{3,2,1,0:T(8,128)(2,1)S(1)}, bf16[3,3,512,512]{3,2,1,0:T(8,128)(2,1)}, u32[]{:S(2)}) %copy-start) | copy-done | bytes 4718616
  2.3 0.0 copy-start.1
  2.3 1.4 %copy-done.1 = bf16[3,512,512]{2,1,0:T(8,128)(2,1)S(1)} copy-done((bf16[3,512,512]{2,1,0:T(8,128)(2,1)S(1)}, bf16[3,512,512]{2,1,0:T(8,128)(2,1)}, u32[]{:S(2)}) %copy-start.1) | copy-done | bytes 1572888
  3.7 0.0 copy-start.2
  3.7 1.4 %copy-done.2 = bf16[512,1536]{1,0:T(8,128)(2,1)S(1)} copy-done((bf16[512,1536]{1,0:T(8,128)(2,1)S(1)}, bf16[512,1536]{1,0:T(8,128)(2,1)}, u32[]{:S(2)}) %copy-start.2) | copy-done | bytes 1572888
  5.2 0.0 copy-start.3
  5.2 1.3 %copy-done.3 = bf16[2,4,160,512]{3,2,1,0:T(8,128)(2,1)S(1)} copy-done((bf16[2,4,160,512]{3,2,1,0:T(8,128)(2,1)S(1)}, bf16[2,4,160,512]{3,2,1,0:T(8,128)(2,1)}, u32[]{:S(2)}) %copy-start.3) | copy-done | bytes 1310744
  6.5 0.0 copy-start.4
  6.5 1.0 %copy-done.4 = bf16[512,512]{1,0:T(8,128)(2,1)S(1)} copy-done((bf16[512,512]{1,0:T(8,128)(2,1)S(1)}, bf16[512,512]{1,0:T(8,128)(2,1)}, u32[]{:S(2)}) %copy-start.4) | copy-done | bytes 524312
  7.5 0.0 copy-start.5
  7.5 0.7 copy-done.5
  8.2 68.2 %shard_map.64 = bf16[2,640,512]{2,1,0:T(8,128)(2,1)S(1)} custom-call(bf16[2,640,512]{2,1,0:T(8,128)(2,1)S(1)} %bitcast.3, s32[16]{0:T(128)S(1)} %copy-done.5, bf16[3,3,512,512]{3,2,1,0:T(8,128)(2,1)S(1)} %copy-done, bf16[3,512,512]{2,1,0:T(8,128)(2,1)S(1)} %copy-done.1, bf16[512,1536]{1,0:T(8,128)(2,1)S(1)} %copy-done.2, bf16[512,512]{1,0:T(8,128)(2,1)S(1)} %copy-done.4), custom_call_target="tpu_custom_call" | custom-call | tf_op jit(solution)/shard_map/pallas_call | solution.py:361
  76.3 1.1 %copy.8 = bf16[2,4,160,512]{3,2,1,0:T(8,128)(2,1)} copy(bf16[2,4,160,512]{3,2,1,0:T(8,128)(2,1)S(1)} %bitcast.2) | data formatting | bytes 2621440
Async XLA Ops:
  0.0 2.3 %copy-start = (bf16[3,3,512,512]{3,2,1,0:T(8,128)(2,1)S(1)}, bf16[3,3,512,512]{3,2,1,0:T(8,128)(2,1)}, u32[]{:S(2)}) copy-start(bf16[3,3,512,512]{3,2,1,0:T(8,128)(2,1)} %ws_hbm.1) | copy-start | bytes 14155780
  2.3 1.4 %copy-start.1 = (bf16[3,512,512]{2,1,0:T(8,128)(2,1)S(1)}, bf16[3,512,512]{2,1,0:T(8,128)(2,1)}, u32[]{:S(2)}) copy-start(bf16[3,512,512]{2,1,0:T(8,128)(2,1)} %wt_hbm.1) | copy-start | bytes 4718596
  3.7 1.4 %copy-start.2 = (bf16[512,1536]{1,0:T(8,128)(2,1)S(1)}, bf16[512,1536]{1,0:T(8,128)(2,1)}, u32[]{:S(2)}) copy-start(bf16[512,1536]{1,0:T(8,128)(2,1)} %wqkv_hbm.1) | copy-start | bytes 4718596
  5.2 1.3 %copy-start.3 = (bf16[2,4,160,512]{3,2,1,0:T(8,128)(2,1)S(1)}, bf16[2,4,160,512]{3,2,1,0:T(8,128)(2,1)}, u32[]{:S(2)}) copy-start(bf16[2,4,160,512]{3,2,1,0:T(8,128)(2,1)} %param.6) | copy-start | bytes 3932164
  6.5 1.0 %copy-start.4 = (bf16[512,512]{1,0:T(8,128)(2,1)S(1)}, bf16[512,512]{1,0:T(8,128)(2,1)}, u32[]{:S(2)}) copy-start(bf16[512,512]{1,0:T(8,128)(2,1)} %wo_hbm.1) | copy-start | bytes 1572868
  7.5 0.7 copy-start.5

commit v2 on v1

--- a/solution.py
+++ b/solution.py
@@ -118,8 +118,8 @@
 def kernel(
     n, slabs, row_count, columns, head_count,
     lat_hbm, starts, ws_hbm, wt_hbm, wqkv_hbm, wo_hbm, out_ref,
-    x, ws, wt, wqkv, wo, hid, rx, tx, ret, bias, lag_mask, att,
-    load_sem, halo_send, halo_recv, fwd_send, fwd_recv, back_send, back_recv,
+    x, ws, wt, wqkv, wo, hid, rx, tx, bias, lag_mask, att,
+    load_sem, halo_send, halo_recv, fwd_send, fwd_recv, back_send, back_recv, keep_sem,
 ):
     frames, pixels, channels = lat_hbm.shape
     total = n * frames
@@ -139,22 +139,84 @@
     for other in (up, down):
         pl.semaphore_signal(barrier, inc=1, device_id=(me, other), device_id_type=MESH)
 
+    pieces = [
+        (lat_hbm.at[f], x.at[f, columns : columns + pixels]) for f in range(frames)
+    ]
+    pieces += [(ws_hbm.at[a, b], ws.at[a, b]) for b in range(3) for a in range(3)]
+    early = len(pieces)
+    pieces += [(wt_hbm, wt), (wqkv_hbm, wqkv), (wo_hbm, wo)]
     loads = [
         pltpu.make_async_copy(source, target, load_sem.at[i])
-        for i, (source, target) in enumerate(
-            (
-                (lat_hbm, x.at[:, columns : columns + pixels]),
-                (ws_hbm, ws),
-                (wt_hbm, wt),
-                (wqkv_hbm, wqkv),
-                (wo_hbm, wo),
-            )
-        )
+        for i, (source, target) in enumerate(pieces)
     ]
-    for load in loads:
+    for load in loads[:early]:
         load.start()
 
-    pl.semaphore_wait(barrier, n + 1)
+    def conv_row(r, waits):
+        sums = []
+        for b in range(3):
+            total_b = None
+            for a in range(3):
+                if waits:
+                    waits.pop(0).wait()
+                source = x[:, (r + a) * columns : (r + a + 1) * columns, :]
+                part = jnp.dot(
+                    source.reshape(frames * columns, channels),
+                    ws[a, b],
+                    preferred_element_type=jnp.float32,
+                )
+                total_b = part if total_b is None else total_b + part
+            sums.append(total_b)
+        place = lax.broadcasted_iota(jnp.int32, (columns, channels), 0)
+        for f in range(frames):
+            part = [s[f * columns : (f + 1) * columns] for s in sums]
+            left = jnp.where(place == 0, 0.0, pltpu.roll(part[0], 1, 0))
+            right = jnp.where(place == columns - 1, 0.0, pltpu.roll(part[2], columns - 1, 0))
+            v = part[1] + left + right
+            hid[f, r * columns : (r + 1) * columns, :] = (
+                v / (1.0 + jnp.exp(-v))
+            ).astype(jnp.bfloat16)
+
+    def spot(k, owner):
+        return pl.multiple_of(lax.rem(first + n * k + owner, blocks) * BLOCK, BLOCK)
+
+    def forward(k, step):
+        peer = lax.rem(me + step, n)
+        return pltpu.make_async_remote_copy(
+            src_ref=hid.at[:, pl.ds(spot(k, peer), BLOCK), :],
+            dst_ref=rx.at[k, pl.ds(me * frames, frames)],
+            send_sem=fwd_send.at[k, step],
+            recv_sem=fwd_recv.at[k, step],
+            device_id=(peer, slab),
+            device_id_type=MESH,
+        )
+
+    def backward(k, step):
+        peer = lax.rem(me + step, n)
+        return pltpu.make_async_remote_copy(
+            src_ref=tx.at[k, pl.ds(peer * frames, frames)],
+            dst_ref=out_ref.at[:, pl.ds(spot(k, me), BLOCK), :],
+            send_sem=back_send.at[k, step],
+            recv_sem=back_recv.at[k, step],
+            device_id=(peer, slab),
+            device_id_type=MESH,
+        )
+
+    def kept(k):
+        return pltpu.make_async_copy(
+            tx.at[k, pl.ds(me * frames, frames)],
+            out_ref.at[:, pl.ds(spot(k, me), BLOCK), :],
+            keep_sem.at[k],
+        )
+
+    def send_forward(k):
+        for step in range(1, n):
+            forward(k, step).start()
+        rx[k, pl.ds(me * frames, frames)] = hid[:, pl.ds(spot(k, me), BLOCK), :]
+
+    for load in loads[:frames]:
+        load.wait()
+
     halos = [
         pltpu.make_async_remote_copy(
             src_ref=lat_hbm.at[:, pixels - columns : pixels],
@@ -173,8 +235,37 @@
             device_id_type=MESH,
         ),
     ]
-    for halo in halos:
-        halo.start()
+    order = list(range(1, row_count)) + [0]
+    sent = 0
+    waits = loads[frames:early]
+    for place, r in enumerate(order):
+        if place == row_count - 2:
+            for halo in halos:
+                halo.wait()
+
+            @pl.when(slab == 0)
+            def _():
+                x[:, 0:columns] = jnp.zeros((frames, columns, channels), jnp.bfloat16)
+
+            @pl.when(slab == slabs - 1)
+            def _():
+                x[:, columns + pixels : 2 * columns + pixels] = jnp.zeros(
+                    (frames, columns, channels), jnp.bfloat16
+                )
+
+        conv_row(r, waits)
+        if place == 0:
+            pl.semaphore_wait(barrier, n + 1)
+            for halo in halos:
+                halo.start()
+            for load in loads[early:]:
+                load.start()
+        while (sent + 1) * BLOCK * n <= (place + 1) * columns:
+            send_forward(sent)
+            sent += 1
+
+    for load in loads[early:]:
+        load.wait()
 
     ids = []
     for f in range(total):
@@ -196,93 +287,6 @@
     bias[...] = jnp.where(allowed, 0.0, -1e30)
     for lag in range(2):
         lag_mask[lag] = jnp.broadcast_to(lags[lag], (rows, channels)).astype(jnp.bfloat16)
-
-    def conv_row(r):
-        sums = []
-        for b in range(3):
-            total_b = None
-            for a in range(3):
-                source = x[:, pl.ds(pl.multiple_of((r + a) * columns, BLOCK), columns), :]
-                part = jnp.dot(
-                    source.reshape(frames * columns, channels),
-                    ws[a, b],
-                    preferred_element_type=jnp.float32,
-                )
-                total_b = part if total_b is None else total_b + part
-            sums.append(total_b)
-        place = lax.broadcasted_iota(jnp.int32, (columns, channels), 0)
-        for f in range(frames):
-            part = [s[f * columns : (f + 1) * columns] for s in sums]
-            left = jnp.where(place == 0, 0.0, pltpu.roll(part[0], 1, 0))
-            right = jnp.where(place == columns - 1, 0.0, pltpu.roll(part[2], columns - 1, 0))
-            v = part[1] + left + right
-            hid[f, pl.ds(pl.multiple_of(r * columns, BLOCK), columns), :] = (
-                v / (1.0 + jnp.exp(-v))
-            ).astype(jnp.bfloat16)
-
-    def spot(k, owner):
-        return pl.multiple_of(lax.rem(first + n * k + owner, blocks) * BLOCK, BLOCK)
-
-    def forward(k, step):
-        peer = lax.rem(me + step, n)
-        return pltpu.make_async_remote_copy(
-            src_ref=hid.at[:, pl.ds(spot(k, peer), BLOCK), :],
-            dst_ref=rx.at[k, pl.ds(me * frames, frames)],
-            send_sem=fwd_send.at[k, step],
-            recv_sem=fwd_recv.at[k, step],
-            device_id=(peer, slab),
-            device_id_type=MESH,
-        )
-
-    def backward(k, step):
-        peer = lax.rem(me + step, n)
-        return pltpu.make_async_remote_copy(
-            src_ref=tx.at[k, pl.ds(peer * frames, frames)],
-            dst_ref=ret.at[:, pl.ds(spot(k, me), BLOCK), :],
-            send_sem=back_send.at[k, step],
-            recv_sem=back_recv.at[k, step],
-            device_id=(peer, slab),
-            device_id_type=MESH,
-        )
-
-    def send_forward(k):
-        for step in range(1, n):
-            forward(k, step).start()
-        rx[k, pl.ds(me * frames, frames)] = hid[:, pl.ds(spot(k, me), BLOCK), :]
-
-    inner = (row_count - 2) * columns // (BLOCK * n)
-    loads[0].wait()
-    loads[1].wait()
-
-    @pl.loop(0, row_count - 2)
-    def _(t):
-        conv_row(t + 1)
-
-    for k in range(inner):
-        send_forward(k)
-    for halo in halos:
-        halo.wait()
-
-    @pl.when(slab == 0)
-    def _():
-        x[:, 0:columns] = jnp.zeros((frames, columns, channels), jnp.bfloat16)
-
-    @pl.when(slab == slabs - 1)
-    def _():
-        x[:, columns + pixels : 2 * columns + pixels] = jnp.zeros(
-            (frames, columns, channels), jnp.bfloat16
-        )
-
-    @pl.loop(0, 2)
-    def _(t):
-        conv_row((1 - t) * (row_count - 1))
-
-    @pl.loop(inner, chunks)
-    def _(k):
-        send_forward(k)
-
-    for load in loads[2:]:
-        load.wait()
 
     lanes = 2 * (channels // head_count)
     low = lax.broadcasted_iota(jnp.int32, (rows, lanes), 1) < lanes // 2
@@ -331,17 +335,13 @@
         tx[k] = result.astype(jnp.bfloat16).reshape(total, BLOCK, channels)
         for step in range(1, n):
             backward(k, step).start()
-        ret[:, pl.ds(spot(k, me), BLOCK), :] = tx[k, pl.ds(me * frames, frames)]
+        kept(k).start()
 
     @pl.loop(0, chunks)
     def _(k):
         for step in range(1, n):
             backward(k, step).wait_recv()
-        for owner in range(n):
-            here = spot(k, owner)
-            moved = x[:, pl.ds(here + columns, BLOCK), :].astype(jnp.float32)
-            moved = moved + ret[:, pl.ds(here, BLOCK), :].astype(jnp.float32)
-            out_ref[:, pl.ds(here, BLOCK), :] = moved.astype(jnp.bfloat16)
+        kept(k).wait()
 
     @pl.loop(0, chunks)
     def _(k):
@@ -362,11 +362,11 @@
         functools.partial(kernel, n, slabs, row_count, columns, HEADS),
         out_shape=jax.ShapeDtypeStruct((frames, pixels, channels), bf16),
         in_specs=[
-            pl.BlockSpec(memory_space=pl.ANY),
+            pl.BlockSpec(memory_space=pltpu.HBM),
             pl.BlockSpec(memory_space=pltpu.SMEM),
         ]
-        + [pl.BlockSpec(memory_space=pl.ANY)] * 4,
-        out_specs=pl.BlockSpec(memory_space=pltpu.VMEM),
+        + [pl.BlockSpec(memory_space=pltpu.HBM)] * 4,
+        out_specs=pl.BlockSpec(memory_space=pltpu.HBM),
         scratch_shapes=[
             pltpu.VMEM((frames, pixels + 2 * columns, channels), bf16),
             pltpu.VMEM(w_space.shape, bf16),
@@ -376,23 +376,24 @@
             pltpu.VMEM((frames, pixels, channels), bf16),
             pltpu.VMEM((chunks, total, BLOCK, channels), bf16),
             pltpu.VMEM((chunks, total, BLOCK, channels), bf16),
-            pltpu.VMEM((frames, pixels, channels), bf16),
             pltpu.VMEM((rows, rows), jnp.float32),
             pltpu.VMEM((2, rows, channels), bf16),
             pltpu.VMEM((rows, channels), bf16),
-            pltpu.SemaphoreType.DMA((5,)),
+            pltpu.SemaphoreType.DMA((frames + 12,)),
             pltpu.SemaphoreType.DMA((2,)),
             pltpu.SemaphoreType.DMA((2,)),
             pltpu.SemaphoreType.DMA((chunks, n)),
             pltpu.SemaphoreType.DMA((chunks, n)),
             pltpu.SemaphoreType.DMA((chunks, n)),
             pltpu.SemaphoreType.DMA((chunks, n)),
+            pltpu.SemaphoreType.DMA((chunks,)),
         ],
         compiler_params=pltpu.CompilerParams(
-            collective_id=0, has_side_effects=True, vmem_limit_bytes=40 * 2**20
+            collective_id=0, has_side_effects=True, vmem_limit_bytes=54 * 2**20
         ),
     )(latents.reshape(frames, pixels, channels), clip_starts, w_space, w_time, w_qkv, w_out)
-    return out.reshape(latents.shape)
+    returned = out.reshape(latents.shape)
+    return (latents.astype(jnp.float32) + returned.astype(jnp.float32)).astype(bf16)
 
 
 def on_device(latents, clip_starts, w_space, w_time, w_qkv, w_out):

time: 77.7 us -> 69.6 us (0.90)
  local copies, waits for them, and re-layouts: 9.22 us -> 0.01 us
  other arithmetic: 0 us -> 2.77 us
  Pallas kernels: 68.2 us -> 66.7 us
    unnamed x13 -> x2, local copies, waits for them, and re-layouts: 9.22 us -> 0.01 us
    convert_element_type x0 -> x1, other arithmetic: none -> 2.77 us  [fused(): (latents.astype(jnp.float32) + returned.astype(jnp.float32)).astype(bf16)]
    pallas_call x1, Pallas kernels: 68.2 us -> 66.7 us  [fused(): pl.pallas_call(functools.partial(kernel, n, slabs, row_count, columns, HE...]
where the time goes in v2:
time: 69.6 us; the launch traced here: 69.5 us
  Pallas kernels  66.7 us (96%)
  other arithmetic  2.77 us (4%)
    pallas_call x1, Pallas kernels, fused(): pl.pallas_call(functools.partial(kernel, n, slabs, row_count, columns, HE...  66.7 us
    convert_element_type x1, other arithmetic, fused(): (latents.astype(jnp.float32) + returned.astype(jnp.float32)).astype(bf16)  2.77 us

profile of v2, /device:TPU:0, one launch (start us, length us, event | category | flops | bytes accessed | tf_op | source)
XLA Modules:
  0.0 69.5 jit_solution(1104663066501291080)
XLA Ops:
  0.0 0.0 copy-start
  0.0 66.7 %shard_map.64 = bf16[2,640,512]{2,1,0:T(8,128)(2,1)} custom-call(bf16[2,640,512]{2,1,0:T(8,128)(2,1)} %bitcast.3, s32[16]{0:T(128)} %starts.1, bf16[3,3,512,512]{3,2,1,0:T(8,128)(2,1)} %ws_hbm.1, bf16[3,512,512]{2,1,0:T(8,128)(2,1)} %wt_hbm.1, bf16[512,1536]{1,0:T(8,128)(2,1)} %wqkv_hbm.1, bf16[512,512]{1,0:T(8,128)(2,1)} %wo_hbm.1), custom_call_target="tpu_custom_call" | custom-call | tf_op jit(solution)/shard_map/pallas_call | solution.py:361
  66.7 0.0 copy-done
  66.7 2.8 %fusion = bf16[2,4,160,512]{3,2,1,0:T(8,128)(2,1)} fusion(bf16[2,4,160,512]{3,2,1,0:T(8,128)(2,1)} %bitcast.4, bf16[2,4,160,512]{3,2,1,0:T(8,128)(2,1)S(1)} %copy-done), kind=kLoop, calls=%fused_computation.1 | loop fusion | flops 2621440 | bytes 3932160 | tf_op jit(solution)/shard_map/convert_element_type | solution.py:396
Async XLA Ops:
  0.0 66.7 %copy-start = (bf16[2,4,160,512]{3,2,1,0:T(8,128)(2,1)S(1)}, bf16[2,4,160,512]{3,2,1,0:T(8,128)(2,1)}, u32[]{:S(2)}) copy-start(bf16[2,4,160,512]{3,2,1,0:T(8,128)(2,1)} %param.6) | copy-start | bytes 3932164

commit v3 on v2

--- a/solution.py
+++ b/solution.py
@@ -118,8 +118,8 @@
 def kernel(
     n, slabs, row_count, columns, head_count,
     lat_hbm, starts, ws_hbm, wt_hbm, wqkv_hbm, wo_hbm, out_ref,
-    x, ws, wt, wqkv, wo, hid, rx, tx, bias, lag_mask, att,
-    load_sem, halo_send, halo_recv, fwd_send, fwd_recv, back_send, back_recv, keep_sem,
+    x, ws, wt, wqkv, wo, hid, rx, tx, ret, bias, lag_mask, att,
+    load_sem, halo_send, halo_recv, fwd_send, fwd_recv, back_send, back_recv,
 ):
     frames, pixels, channels = lat_hbm.shape
     total = n * frames
@@ -195,18 +195,11 @@
         peer = lax.rem(me + step, n)
         return pltpu.make_async_remote_copy(
             src_ref=tx.at[k, pl.ds(peer * frames, frames)],
-            dst_ref=out_ref.at[:, pl.ds(spot(k, me), BLOCK), :],
+            dst_ref=ret.at[:, pl.ds(spot(k, me), BLOCK), :],
             send_sem=back_send.at[k, step],
             recv_sem=back_recv.at[k, step],
             device_id=(peer, slab),
             device_id_type=MESH,
-        )
-
-    def kept(k):
-        return pltpu.make_async_copy(
-            tx.at[k, pl.ds(me * frames, frames)],
-            out_ref.at[:, pl.ds(spot(k, me), BLOCK), :],
-            keep_sem.at[k],
         )
 
     def send_forward(k):
@@ -335,13 +328,17 @@
         tx[k] = result.astype(jnp.bfloat16).reshape(total, BLOCK, channels)
         for step in range(1, n):
             backward(k, step).start()
-        kept(k).start()
+        ret[:, pl.ds(spot(k, me), BLOCK), :] = tx[k, pl.ds(me * frames, frames)]
 
     @pl.loop(0, chunks)
     def _(k):
         for step in range(1, n):
             backward(k, step).wait_recv()
-        kept(k).wait()
+        for owner in range(n):
+            here = spot(k, owner)
+            moved = x[:, pl.ds(here + columns, BLOCK), :].astype(jnp.float32)
+            moved = moved + ret[:, pl.ds(here, BLOCK), :].astype(jnp.float32)
+            out_ref[:, pl.ds(here, BLOCK), :] = moved.astype(jnp.bfloat16)
 
     @pl.loop(0, chunks)
     def _(k):
@@ -358,6 +355,7 @@
     chunks = pixels // (BLOCK * n)
     rows = total * BLOCK
     bf16 = jnp.bfloat16
+    hbm = functools.partial(pltpu.with_memory_space_constraint, memory_space=pltpu.HBM)
     out = pl.pallas_call(
         functools.partial(kernel, n, slabs, row_count, columns, HEADS),
         out_shape=jax.ShapeDtypeStruct((frames, pixels, channels), bf16),
@@ -366,7 +364,7 @@
             pl.BlockSpec(memory_space=pltpu.SMEM),
         ]
         + [pl.BlockSpec(memory_space=pltpu.HBM)] * 4,
-        out_specs=pl.BlockSpec(memory_space=pltpu.HBM),
+        out_specs=pl.BlockSpec(memory_space=pltpu.VMEM),
         scratch_shapes=[
             pltpu.VMEM((frames, pixels + 2 * columns, channels), bf16),
             pltpu.VMEM(w_space.shape, bf16),
@@ -376,6 +374,7 @@
             pltpu.VMEM((frames, pixels, channels), bf16),
             pltpu.VMEM((chunks, total, BLOCK, channels), bf16),
             pltpu.VMEM((chunks, total, BLOCK, channels), bf16),
+            pltpu.VMEM((frames, pixels, channels), bf16),
             pltpu.VMEM((rows, rows), jnp.float32),
             pltpu.VMEM((2, rows, channels), bf16),
             pltpu.VMEM((rows, channels), bf16),
@@ -386,14 +385,16 @@
             pltpu.SemaphoreType.DMA((chunks, n)),
             pltpu.SemaphoreType.DMA((chunks, n)),
             pltpu.SemaphoreType.DMA((chunks, n)),
-            pltpu.SemaphoreType.DMA((chunks,)),
         ],
         compiler_params=pltpu.CompilerParams(
-            collective_id=0, has_side_effects=True, vmem_limit_bytes=54 * 2**20
+            collective_id=0, has_side_effects=True, vmem_limit_bytes=40 * 2**20
         ),
-    )(latents.reshape(frames, pixels, channels), clip_starts, w_space, w_time, w_qkv, w_out)
-    returned = out.reshape(latents.shape)
-    return (latents.astype(jnp.float32) + returned.astype(jnp.float32)).astype(bf16)
+    )(
+        hbm(latents.reshape(frames, pixels, channels)),
+        hbm(clip_starts),
+        *(hbm(weight) for weight in (w_space, w_time, w_qkv, w_out)),
+    )
+    return out.reshape(latents.shape)
 
 
 def on_device(latents, clip_starts, w_space, w_time, w_qkv, w_out):

time: 69.6 us -> 67.7 us (0.973)
  other arithmetic: 2.77 us -> 0 us
  local copies, waits for them, and re-layouts: 0.01 us -> 1.06 us
    convert_element_type x1 -> x0, other arithmetic: 2.77 us -> none  [fused(): (latents.astype(jnp.float32) + returned.astype(jnp.float32)).astype(bf16)]
    unnamed x2 -> x1, local copies, waits for them, and re-layouts: 0.01 us -> 1.06 us
where the time goes in v3:
time: 67.7 us; the launch traced here: 67.6 us
  Pallas kernels  66.5 us (98%)
  local copies, waits for them, and re-layouts  1.06 us (2%)
    pallas_call x1, Pallas kernels, fused(): pl.pallas_call(functools.partial(kernel, n, slabs, row_count, columns, HE...  66.5 us

profile of v3, /device:TPU:0, one launch (start us, length us, event | category | flops | bytes accessed | tf_op | source)
XLA Modules:
  0.0 67.6 jit_solution(10142548812393666629)
XLA Ops:
  0.0 66.5 %shard_map.64 = bf16[2,640,512]{2,1,0:T(8,128)(2,1)S(1)} custom-call(bf16[2,640,512]{2,1,0:T(8,128)(2,1)} %bitcast.3, s32[16]{0:T(128)} %starts.1, bf16[3,3,512,512]{3,2,1,0:T(8,128)(2,1)} %ws_hbm.1, bf16[3,512,512]{2,1,0:T(8,128)(2,1)} %wt_hbm.1, bf16[512,1536]{1,0:T(8,128)(2,1)} %wqkv_hbm.1, bf16[512,512]{1,0:T(8,128)(2,1)} %wo_hbm.1), custom_call_target="tpu_custom_call" | custom-call | tf_op jit(solution)/shard_map/pallas_call | solution.py:359
  66.5 1.1 %copy.8 = bf16[2,4,160,512]{3,2,1,0:T(8,128)(2,1)} copy(bf16[2,4,160,512]{3,2,1,0:T(8,128)(2,1)S(1)} %bitcast.2) | data formatting | bytes 2621440
